TPU v7x, 32 devices: a whole 2x2x4 slice. The times are simulated.
32 devices in a mesh: section: 4 (over y, x), orient: 8 (over z, core).
Axes of the slice: x: 2, y: 2, z: 4, core: 2. Of those that a mesh axis runs over, the one named last changes fastest.
Arguments:
- patterns: bfloat16 [4, 128, 65536], P('section', None, 'orient'), may hold values from -6 to 6
- detector_gain: float32 [65536], P('orient'), may hold values from 0.1 to 1.9
- background: float32 [65536], P('orient'), may hold values from -6 to 6
- bin_map: int32 [65536], P('orient'), may hold values from 0 to 12287, as said below
- templates: bfloat16 [12800, 12288], P(('section', 'orient')), may hold values from -0.0546875 to 0.0546875
- best_picks: int32 [4, 128], replicated, may hold values from 0 to 12799
Outputs:
- top_scores: float32 [4, 128, 8], P('section')
- refined: float32 [4, 128, 3], P('section', 'orient')
Inputs may be any that keep to these rules, and one draw needn't show every extreme that they name: `bin_map`: each pixel's polar bin r * 192 + a, with r given by the pixel's distance and a by its direction from a beam centre near the middle of the square detector.
All inputs are finite; a program needn't handle non-finite values.
Results may differ from a plain program's by a relative error of at most 0.0065.
Values may be sent and summed in bfloat16 or wider, within the bound.
No kernel may reach another device: no remote copies, remote signals or barrier semaphores. Data moves between devices by JAX's collectives and lax.ppermute only.
A program may use at most 256 MiB of HBM per device.

v0:
```python
import jax
import jax.numpy as jnp
from jax import lax
from jax.sharding import PartitionSpec as P

RAD = 64
ANG = 192
TOPK = 8
REACH = 1


EPS = 1e-06
BLOCK_ROWS = 512


def shifted(x, axis, by):
    count = lax.axis_size(axis)
    return lax.ppermute(x, axis, [(i, (i + by) % count) for i in range(count)])


def merged_2(part, axis, combine):
    gathered = lax.all_gather(part, axis)

    def take(source):
        return lax.dynamic_index_in_dim(gathered, source, 0, False)

    return lax.fori_loop(
        1, lax.axis_size(axis), lambda source, state: combine(state, take(source)), take(0)
    )


def bin_block(corrected, bin_map, first, length):
    targets = first + lax.iota(jnp.int32, length)
    onehot = (bin_map[None, :] == targets[:, None]).astype(jnp.bfloat16)
    return lax.dot_general(
        onehot, corrected, (((1,), (1,)), ((), ())), preferred_element_type=jnp.float32
    )


def bin_rows(corrected, bin_map, length):
    blocks = 1
    while length // blocks > BLOCK_ROWS and length % (2 * blocks) == 0:
        blocks = blocks * 2
    height = length // blocks
    starts = height * lax.iota(jnp.int32, blocks)
    stacked = lax.map(lambda begin: bin_block(corrected, bin_map, begin, height), starts)
    return stacked.reshape(length, corrected.shape[0])


def merge_best(first_best, second_best):
    return lax.top_k(jnp.concatenate([first_best, second_best], axis=-1), TOPK)[0]


def score_batch(features, templates, wanted, group_base):
    scores = lax.dot_general(
        features, templates, (((0,), (1,)), ((), ())), preferred_element_type=jnp.float32
    )
    best = lax.top_k(scores, TOPK)[0]
    local = wanted - group_base
    count = templates.shape[0]
    owned = (local >= 0) & (local < count)
    chosen = jnp.take(templates, jnp.clip(local, 0, count - 1), axis=0)
    width = features.shape[1]
    chosen = chosen.reshape(width, RAD, ANG)
    grid = features.T.reshape(width, RAD, ANG)
    columns = []
    for offset in range(-REACH, REACH + 1):
        rolled = jnp.roll(chosen, -offset, axis=2)
        columns.append(jnp.sum(grid.astype(jnp.float32) * rolled.astype(jnp.float32), axis=(1, 2)))
    refined = jnp.where(owned[:, None], jnp.stack(columns, axis=1), 0.0)
    return (best, refined)


def body(patterns, detector_gain, background, bin_map, templates, best_picks):
    sections = lax.axis_size("section")
    orients = lax.axis_size("orient")
    section_index = lax.axis_index("section")
    orient_index = lax.axis_index("orient")
    features_total = RAD * ANG
    corrected = ((patterns[0].astype(jnp.float32) - background) * detector_gain).astype(
        jnp.bfloat16
    )
    whole = lax.psum(bin_rows(corrected, bin_map, features_total), "orient")
    squares = jnp.sum(whole * whole, axis=0)
    features = (whole * lax.rsqrt(squares / features_total + EPS)).astype(jnp.bfloat16)
    group_base = (section_index * orients + orient_index) * templates.shape[0]
    held = features
    running_best = None
    running_refined = None
    for turn in range(sections):
        batch = (section_index + sections - turn) % sections
        wanted = lax.dynamic_index_in_dim(best_picks, batch, 0, keepdims=False)
        best, refined = score_batch(held, templates, wanted, group_base)
        if turn > 0:
            best = merge_best(running_best, best)
            refined = running_refined + refined
        packed = shifted(jnp.concatenate([best, refined], axis=1), "section", 1)
        running_best = packed[:, :TOPK]
        running_refined = packed[:, TOPK:]
        if turn + 1 < sections:
            held = shifted(held, "section", 1)
    merged = merged_2(running_best, "orient", merge_best)
    shares = lax.psum_scatter(running_refined, "orient", scatter_dimension=0, tiled=True)
    return (merged[None], shares[None])


def solution(mesh):
    return jax.shard_map(
        body,
        mesh=mesh,
        in_specs=(
            P("section", None, "orient"),
            P("orient"),
            P("orient"),
            P("orient"),
            P(("section", "orient"), None),
            P(),
        ),
        out_specs=(P("section", None, None), P("section", "orient", None)),
        check_vma=False,
    )
```

profile of v0, /device:TPU:0, one launch (start us, length us, event | category | flops | bytes accessed | tf_op | source)
XLA Modules:
  0.0 587.0 jit_solution(10107045473070248577)
XLA Ops:
  9.4 122.0 %while.25 = (s32[]{:T(128)}, f32[32,384,128]{2,1,0:T(8,128)}, s32[8192]{0:T(1024)S(1)}, s32[32]{0:T(128)S(1)}, bf16[128,8192]{1,0:T(8,128)(2,1)S(1)}, /*index=5*/s32[]{:T(128)}) while((s32[]{:T(128)}, f32[32,384,128]{2,1,0:T(8,128)}, s32[8192]{0:T(1024)S(1)}, s32[32]{0:T(128)S(1)}, bf16[128,8192]{1,0:T(8,128)(2,1)S(1)}, ...), condition=%wide.region_1.2_spmd, body=%wide.region_0.1_spmd.sunk | while | flops 808452480 | bytes 2330197 | solution.py:46
  131.4 6.6 %copy.76 = f32[12288,128]{0,1:T(8,128)} copy(f32[12288,128]{1,0:T(8,128)} %bitcast.142) | data formatting | bytes 12582912 | tf_op jit(solution)/shard_map/reshape | solution.py:47
  138.7 10.4 %gather_fusion = bf16[128,12288]{1,0:T(8,128)(2,1)S(1)} fusion(bf16[400,12288]{1,0:T(8,128)(2,1)} %param.16, s32[1024]{0:T(1024)S(1)} %get-tuple-element.223), kind=kCustom, calls=%fused_computation.clone | custom fusion | bytes 6291968 | tf_op jit(solution)/shard_map/jit(_take)/gather | solution.py:62
  160.8 10.4 %gather_fusion.1 = bf16[128,12288]{1,0:T(8,128)(2,1)S(1)} fusion(bf16[400,12288]{1,0:T(8,128)(2,1)} %param.16, s32[1024]{0:T(1024)S(1)} %get-tuple-element.222), kind=kCustom, calls=%fused_computation.1.clone | custom fusion | bytes 6291968 | tf_op jit(solution)/shard_map/jit(_take)/gather | solution.py:62
  183.1 10.5 %gather_fusion.2 = bf16[128,12288]{1,0:T(8,128)(2,1)S(1)} fusion(bf16[400,12288]{1,0:T(8,128)(2,1)} %param.16, s32[1024]{0:T(1024)S(1)} %get-tuple-element.221), kind=kCustom, calls=%fused_computation.2.clone | custom fusion | bytes 6291968 | tf_op jit(solution)/shard_map/jit(_take)/gather | solution.py:62
  205.2 10.5 %gather_fusion.3 = bf16[128,12288]{1,0:T(8,128)(2,1)S(1)} fusion(bf16[400,12288]{1,0:T(8,128)(2,1)} %param.16, s32[1024]{0:T(1024)S(1)} %get-tuple-element.220), kind=kCustom, calls=%fused_computation.3.clone | custom fusion | bytes 6291968 | tf_op jit(solution)/shard_map/jit(_take)/gather | solution.py:62
  251.6 6.6 %copy.54 = f32[128,12288]{1,0:T(8,128)} copy(f32[128,12288]{0,1:T(8,128)} %bitcast_convert_fusion.6) | data formatting | bytes 12582912 | tf_op jit(solution)/shard_map/convert_element_type | solution.py:69
  258.3 6.7 %copy.53 = f32[128,12288]{1,0:T(8,128)} copy(f32[128,12288]{0,1:T(8,128)} %bitcast_convert_fusion.7) | data formatting | bytes 12582912 | tf_op jit(solution)/shard_map/convert_element_type | solution.py:69
  280.4 10.2 %fusion.19 = (f32[128]{0:T(128)}, f32[128]{0:T(128)}, f32[128]{0:T(128)}, bf16[12288,128]{0,1:T(8,128)(2,1)}) fusion(f32[128,12288]{1,0:T(8,128)} %copy.53, f32[128,12288]{1,0:T(8,128)} %copy.54, f32[12288,128]{0,1:T(8,128)} %all-reduce.2.cloned.1.call-done, f32[128]{0:T(128)S(1)} %add_rsqrt_fusion, bf16[128,12288]{1,0:T(8,128)(2,1)S(1)} %copy-done.7, ...), kind=kLoop, calls=%fused_computation.34 | loop fusion | flops 17301120 | bytes 25168000 | tf_op jit(solution)/shard_map/reduce_sum | solution.py:69
  299.9 7.6 %top_k.60 = (f32[128,400]{0,1:T(8,128)}, s32[128,400]{0,1:T(8,128)}) sort(f32[128,400]{0,1:T(8,128)S(1)} %fusion.36, s32[128,400]{0,1:T(8,128)S(1)} %iota.33.clone), dimensions={1}, to_apply=%region_4.5 | sort | flops 819200 | bytes 819200 | tf_op jit(solution)/shard_map/top_k | solution.py:58
  312.4 49.1 %collective-permute-done.1 = bf16[12288,128]{0,1:T(8,128)(2,1)} collective-permute-done((bf16[12288,128]{0,1:T(8,128)(2,1)}, bf16[12288,128]{0,1:T(8,128)(2,1)}, u32[]{:S(2)}, u32[]{:S(2)}) %collective-permute-start.1) | collective-permute-done | bytes 3145760 | tf_op jit(solution)/shard_map/ppermute | solution.py:18
  386.3 7.7 %top_k.62 = (f32[128,400]{0,1:T(8,128)}, s32[128,400]{0,1:T(8,128)}) sort(f32[128,400]{0,1:T(8,128)S(1)} %fusion.37, s32[128,400]{0,1:T(8,128)S(1)} %iota.33.clone), dimensions={1}, to_apply=%region_8.10 | sort | flops 819200 | bytes 819200 | tf_op jit(solution)/shard_map/top_k | solution.py:58
  398.1 6.8 %fusion.16 = (f32[128]{0:T(128)S(1)}, f32[128]{0:T(128)S(1)}, f32[128]{0:T(128)S(1)}) fusion(f32[128,12288]{1,0:T(8,128)} %copy.59, bf16[12288,128]{0,1:T(8,128)(2,1)} %collective-permute-done.1, f32[128,12288]{1,0:T(8,128)} %copy.60, bf16[128,12288]{1,0:T(8,128)(2,1)S(1)} %copy-done.5, pred[128]{0:T(512)(128)(4,1)} %copy-done.26), kind=kLoop, calls=%fused_computation.28 | loop fusion | flops 14155392 | bytes 18876032 | tf_op jit(solution)/shard_map/reduce_sum | solution.py:69
  410.1 6.7 %copy.64 = f32[128,12288]{1,0:T(8,128)} copy(f32[128,12288]{0,1:T(8,128)} %bitcast_convert_fusion.3) | data formatting | bytes 12582912 | tf_op jit(solution)/shard_map/convert_element_type | solution.py:69
  423.4 8.2 %collective-permute-done.2 = f32[128,11]{0,1:T(8,128)S(1)} collective-permute-done((f32[128,11]{0,1:T(8,128)S(1)}, f32[128,11]{0,1:T(8,128)S(1)}, u32[]{:S(2)}, u32[]{:S(2)}) %collective-permute-start.2) | collective-permute-done | bytes 5664 | tf_op jit(solution)/shard_map/ppermute | solution.py:18
  438.8 7.6 %top_k.70 = (f32[128,400]{0,1:T(8,128)}, s32[128,400]{0,1:T(8,128)}) sort(f32[128,400]{0,1:T(8,128)S(1)} %fusion.38, s32[128,400]{0,1:T(8,128)S(1)} %iota.33.clone), dimensions={1}, to_apply=%region_13.15 | sort | flops 819200 | bytes 819200 | tf_op jit(solution)/shard_map/top_k | solution.py:58
  449.1 6.7 %fusion.13 = (f32[128]{0:T(128)S(1)}, f32[128]{0:T(128)S(1)}, f32[128]{0:T(128)S(1)}) fusion(f32[128,12288]{1,0:T(8,128)} %copy.64, bf16[12288,128]{0,1:T(8,128)(2,1)} %collective-permute-done.3, f32[128,12288]{1,0:T(8,128)} %copy.65, bf16[128,12288]{1,0:T(8,128)(2,1)S(1)} %copy-done.3, pred[128]{0:T(512)(128)(4,1)} %copy-done.25), kind=kLoop, calls=%fused_computation.22 | loop fusion | flops 14155392 | bytes 18876032 | tf_op jit(solution)/shard_map/reduce_sum | solution.py:69
  463.9 6.6 %copy.69 = f32[128,12288]{1,0:T(8,128)} copy(f32[128,12288]{0,1:T(8,128)} %bitcast_convert_fusion.1) | data formatting | bytes 12582912 | tf_op jit(solution)/shard_map/convert_element_type | solution.py:69
  470.5 6.6 %copy.70 = f32[128,12288]{1,0:T(8,128)} copy(f32[128,12288]{0,1:T(8,128)} %bitcast_convert_fusion) | data formatting | bytes 12582912 | tf_op jit(solution)/shard_map/convert_element_type | solution.py:69
  477.1 41.2 %collective-permute-done.4 = f32[128,11]{0,1:T(8,128)S(1)} collective-permute-done((f32[128,11]{0,1:T(8,128)S(1)}, f32[128,11]{0,1:T(8,128)S(1)}, u32[]{:S(2)}, u32[]{:S(2)}) %collective-permute-start.4) | collective-permute-done | bytes 5664 | tf_op jit(solution)/shard_map/ppermute | solution.py:18
  525.5 7.6 %top_k.74 = (f32[128,400]{0,1:T(8,128)}, s32[128,400]{0,1:T(8,128)}) sort(f32[128,400]{0,1:T(8,128)S(1)} %fusion.39, s32[128,400]{0,1:T(8,128)S(1)} %iota.33.clone), dimensions={1}, to_apply=%region_18.20 | sort | flops 819200 | bytes 819200 | tf_op jit(solution)/shard_map/top_k | solution.py:58
  535.7 6.7 %fusion.10 = (f32[128]{0:T(128)S(1)}, f32[128]{0:T(128)S(1)}, f32[128]{0:T(128)S(1)}) fusion(f32[128,12288]{1,0:T(8,128)} %copy.69, bf16[12288,128]{0,1:T(8,128)(2,1)} %collective-permute-done.5, f32[128,12288]{1,0:T(8,128)} %copy.70, bf16[128,12288]{1,0:T(8,128)(2,1)S(1)} %copy-done.1, pred[128]{0:T(512)(128)(4,1)} %copy-done.24), kind=kLoop, calls=%fused_computation.16 | loop fusion | flops 14155392 | bytes 18876032 | tf_op jit(solution)/shard_map/reduce_sum | solution.py:69
  548.5 14.0 %all-gather = f32[1024,8]{0,1:T(8,128)S(1)} all-gather(f32[128,8]{0,1:T(8,128)S(1)} %slice.147), channel_id=2, replica_groups=mesh['section'=4,'orient'=8] {'orient'}, dimensions={0}, use_global_device_ids=true | all-gather | bytes 36864 | tf_op jit(solution)/shard_map/all_gather | solution.py:22
  567.7 11.0 %reduce-scatter.4.cloned.1.call-done = f32[16,3]{1,0:T(8,128)} async-done(((f32[128,3]{1,0:T(8,128)}), f32[16,3]{1,0:T(8,128)}) %reduce-scatter.4.cloned.1.call-update) | async-done | bytes 208
  (312 shorter events, 311.0 us)
Async XLA Ops:
  7.2 269.7 %all-reduce.2.cloned.1.call-start = ((), (), s32[]{:S(2)}) async-start(), calls=%async_computation.1 | async-start | bytes 12582912 | tf_op jit(solution)/shard_map/psum | solution.py:83
  138.0 440.6 %reduce-scatter.4.cloned.1.call-start = ((), (), s32[]{:S(2)}) async-start(), calls=%async_computation.2 | async-start | bytes 73728
  138.7 32.6 %copy-start.26 = (pred[128]{0:T(512)(128)(4,1)}, pred[128]{0:T(512)(128)(4,1)S(1)}, u32[]{:S(2)}) copy-start(pred[128]{0:T(512)(128)(4,1)S(1)} %get-tuple-element.214) | copy-start | bytes 388
  138.7 54.9 %copy-start.25 = (pred[128]{0:T(512)(128)(4,1)}, pred[128]{0:T(512)(128)(4,1)S(1)}, u32[]{:S(2)}) copy-start(pred[128]{0:T(512)(128)(4,1)S(1)} %get-tuple-element.216) | copy-start | bytes 388
  138.7 77.1 %copy-start.24 = (pred[128]{0:T(512)(128)(4,1)}, pred[128]{0:T(512)(128)(4,1)S(1)}, u32[]{:S(2)}) copy-start(pred[128]{0:T(512)(128)(4,1)S(1)} %get-tuple-element.185) | copy-start | bytes 388
  270.9 9.4 %copy-start.7 = (bf16[128,12288]{1,0:T(8,128)(2,1)S(1)}, bf16[128,12288]{1,0:T(8,128)(2,1)}, u32[]{:S(2)}) copy-start(bf16[128,12288]{1,0:T(8,128)(2,1)} %copy-done.6) | copy-start | bytes 9437188
  276.9 18.2 %slice-start = ((s8[9830400]{0:T(1024)(128)(4,1)}), s8[4194304]{0:T(1024)(128)(4,1)S(1)}, s32[]{:S(2)}) async-start(s8[9830400]{0:T(1024)(128)(4,1)} %bitcast.132), calls=%async_computation.3 | async-start | bytes 8388608
  280.3 11.7 %copy-start.17 = (bf16[128,64,192]{0,2,1:T(8,128)(2,1)S(1)}, bf16[128,64,192]{0,2,1:T(8,128)(2,1)}, u32[]{:S(2)}) copy-start(bf16[128,64,192]{0,2,1:T(8,128)(2,1)} %pad_maximum_fusion.6) | copy-start | bytes 9437188
  280.3 14.8 %slice-start.1 = ((s8[9830400]{0:T(1024)(128)(4,1)}), s8[4194304]{0:T(1024)(128)(4,1)S(1)}, s32[]{:S(2)}) async-start(s8[9830400]{0:T(1024)(128)(4,1)} %bitcast.132), calls=%async_computation.4 | async-start | bytes 8388608
  280.3 14.8 %slice-start.2 = ((s8[9830400]{0:T(1024)(128)(4,1)}), s8[1441792]{0:T(1024)(128)(4,1)S(1)}, s32[]{:S(2)}) async-start(s8[9830400]{0:T(1024)(128)(4,1)} %bitcast.132), calls=%async_computation.5 | async-start | bytes 2883584
  290.5 71.0 %collective-permute-start.1 = (bf16[12288,128]{0,1:T(8,128)(2,1)}, bf16[12288,128]{0,1:T(8,128)(2,1)}, u32[]{:S(2)}, u32[]{:S(2)}) collective-permute-start(bf16[12288,128]{0,1:T(8,128)(2,1)} %get-tuple-element.191), channel_id=1, source_target_pairs={{0,8},{8,16},{16,24},{24,0},{1,9},{9,17},{17,25},{25,1},{2,10},{10... | collective-permute-start | bytes 9437192 | tf_op jit(solution)/shard_map/ppermute | solution.py:18
  295.1 67.0 %copy-start.9 = (bf16[128,64,192]{0,2,1:T(8,128)(2,1)S(1)}, bf16[128,64,192]{0,2,1:T(8,128)(2,1)}, u32[]{:S(2)}) copy-start(bf16[128,64,192]{0,2,1:T(8,128)(2,1)} %pad_maximum_fusion.7) | copy-start | bytes 9437188
  310.9 67.7 %collective-permute-start = (f32[128,11]{0,1:T(8,128)S(1)}, f32[128,11]{0,1:T(8,128)S(1)}, u32[]{:S(2)}, u32[]{:S(2)}) collective-permute-start(f32[128,11]{0,1:T(8,128)S(1)} %pad_maximum_fusion.9), channel_id=1, source_target_pairs={{0,8},{8,16},{16,24},{24,0},{1,9},{9,17},{17,25},{25,1},{2,10},{10... | collective-permute-start | bytes 16904 | tf_op jit(solution)/shard_map/ppermute | solution.py:18
  361.6 70.7 %collective-permute-start.3 = (bf16[12288,128]{0,1:T(8,128)(2,1)}, bf16[12288,128]{0,1:T(8,128)(2,1)}, u32[]{:S(2)}, u32[]{:S(2)}) collective-permute-start(bf16[12288,128]{0,1:T(8,128)(2,1)} %collective-permute-done.1), channel_id=1, source_target_pairs={{0,8},{8,16},{16,24},{24,0},{1,9},{9,17},{17,25},{25,1},{2,10},{10... | collective-permute-start | bytes 9437192 | tf_op jit(solution)/shard_map/ppermute | solution.py:18
  379.8 18.3 %copy-start.5 = (bf16[128,12288]{1,0:T(8,128)(2,1)S(1)}, bf16[128,12288]{1,0:T(8,128)(2,1)}, u32[]{:S(2)}) copy-start(bf16[128,12288]{1,0:T(8,128)(2,1)} %copy-done.4) | copy-start | bytes 9437188
  398.1 10.0 %copy-start.8 = (bf16[128,64,191]{0,2,1:T(8,128)(2,1)S(1)}, bf16[128,64,191]{0,2,1:T(8,128)(2,1)}, u32[]{:S(2)}) copy-start(bf16[128,64,191]{0,2,1:T(8,128)(2,1)} %get-tuple-element.194) | copy-start | bytes 9388036
  398.1 10.0 %copy-start.20 = (bf16[128,64,1]{0,2,1:T(2,128)(2,1)S(1)}, bf16[128,64,1]{0,2,1:T(2,128)(2,1)}, u32[]{:S(2)}) copy-start(bf16[128,64,1]{0,2,1:T(2,128)(2,1)} %get-tuple-element.196) | copy-start | bytes 49156
  405.6 26.0 %collective-permute-start.2 = (f32[128,11]{0,1:T(8,128)S(1)}, f32[128,11]{0,1:T(8,128)S(1)}, u32[]{:S(2)}, u32[]{:S(2)}) collective-permute-start(f32[128,11]{0,1:T(8,128)S(1)} %pad_maximum_fusion.11), channel_id=1, source_target_pairs={{0,8},{8,16},{16,24},{24,0},{1,9},{9,17},{17,25},{25,1},{2,10},{10... | collective-permute-start | bytes 16904 | tf_op jit(solution)/shard_map/ppermute | solution.py:18
  432.2 16.9 %copy-start.3 = (bf16[128,12288]{1,0:T(8,128)(2,1)S(1)}, bf16[128,12288]{1,0:T(8,128)(2,1)}, u32[]{:S(2)}) copy-start(bf16[128,12288]{1,0:T(8,128)(2,1)} %copy-done.2) | copy-start | bytes 9437188
  449.1 69.9 %collective-permute-start.5 = (bf16[12288,128]{0,1:T(8,128)(2,1)}, bf16[12288,128]{0,1:T(8,128)(2,1)}, u32[]{:S(2)}, u32[]{:S(2)}) collective-permute-start(bf16[12288,128]{0,1:T(8,128)(2,1)} %collective-permute-done.3), channel_id=1, source_target_pairs={{0,8},{8,16},{16,24},{24,0},{1,9},{9,17},{17,25},{25,1},{2,10},{10... | collective-permute-start | bytes 9437192 | tf_op jit(solution)/shard_map/ppermute | solution.py:18
  456.6 61.7 %collective-permute-start.4 = (f32[128,11]{0,1:T(8,128)S(1)}, f32[128,11]{0,1:T(8,128)S(1)}, u32[]{:S(2)}, u32[]{:S(2)}) collective-permute-start(f32[128,11]{0,1:T(8,128)S(1)} %pad_maximum_fusion.13), channel_id=1, source_target_pairs={{0,8},{8,16},{16,24},{24,0},{1,9},{9,17},{17,25},{25,1},{2,10},{10... | collective-permute-start | bytes 16904 | tf_op jit(solution)/shard_map/ppermute | solution.py:18
  518.9 16.8 %copy-start.1 = (bf16[128,12288]{1,0:T(8,128)(2,1)S(1)}, bf16[128,12288]{1,0:T(8,128)(2,1)}, u32[]{:S(2)}) copy-start(bf16[128,12288]{1,0:T(8,128)(2,1)} %copy-done) | copy-start | bytes 9437188
  543.1 4.6 collective-permute-start.6
  567.7 12.3 %copy-start.19 = (f32[128,8]{0,1:T(8,128)}, f32[128,8]{0,1:T(8,128)S(1)}, u32[]{:S(2)}) copy-start(f32[128,8]{0,1:T(8,128)S(1)} %get-tuple-element.142) | copy-start | bytes 12292
  (22 other events, 77.3 us)
Sparse Core Ops, SparseCore 0:
  138.1 138.7 all-reduce.1
  548.6 30.0 reduce-scatter.3
where the time goes:
time: 596 us; the launch traced here: 587 us
  local copies, waits for them, and re-layouts  175 us (29%)
  other arithmetic  147 us (25%)
  waiting for transfers between devices  120 us (20%)
  matrix products  107 us (18%)
  between operations  14.9 us (2%)
  blocking collectives  14 us (2%)
  starting transfers between devices  9.06 us (2%)
    ppermute x7, waiting for transfers between devices, shifted(): return lax.ppermute(x, axis, [(i, (i + by) % count) for i in range(count)])  103 us
    dot_general x32, matrix products, bin_block(): lax.dot_general(onehot, corrected, (((1,), (1,)), ((), ())), preferred_el...  82.4 us
    convert_element_type x8, local copies, waits for them, and re-layouts, score_batch(): rolled.astype(jnp.float32)  53 us
    gather x4, local copies, waits for them, and re-layouts, score_batch(): chosen = jnp.take(templates, jnp.clip(local, 0, count - 1), axis=0)  41.8 us
    top_k x4, other arithmetic, score_batch(): best = lax.top_k(scores, TOPK)[0]  30.5 us
    reduce_sum x4, other arithmetic, score_batch(): jnp.sum(grid.astype(jnp.float32) * rolled.astype(jnp.float32), axis=(1, 2))  30.3 us
    convert_element_type x8, other arithmetic, score_batch(): rolled.astype(jnp.float32)  26.7 us
    unnamed x4, matrix products  24.4 us
  transfers between devices with their start and end apart: 9, of which 6 were waited for; matrix products, arithmetic and copies ran while one was open for 39% of the time, Pallas kernels for 0%

commit v1 on v0

--- a/solution.py
+++ b/solution.py
@@ -1,6 +1,10 @@
+import functools
+
 import jax
 import jax.numpy as jnp
 from jax import lax
+from jax.experimental import pallas as pl
+from jax.experimental.pallas import tpu as pltpu
 from jax.sharding import PartitionSpec as P
 
 RAD = 64
@@ -71,7 +75,7 @@
     return (best, refined)
 
 
-def body(patterns, detector_gain, background, bin_map, templates, best_picks):
+def dense_body(patterns, detector_gain, background, bin_map, templates, best_picks):
     sections = lax.axis_size("section")
     orients = lax.axis_size("orient")
     section_index = lax.axis_index("section")
@@ -104,9 +108,531 @@
     return (merged[None], shares[None])
 
 
+BINS = RAD * ANG
+SEG = 1792
+SEGS = 6
+ROOM = 2 * SEG
+TILE = 256
+WINDOW = 256
+KEPT = 32
+PAIR = 2 * ANG
+MIB = 1 << 20
+F32 = jnp.float32
+BF16 = jnp.bfloat16
+
+
+def vmem():
+    return pl.BlockSpec(memory_space=pltpu.VMEM)
+
+
+def smem():
+    return pl.BlockSpec(memory_space=pltpu.SMEM)
+
+
+def dot_nt(a, b):
+    return lax.dot_general(a, b, (((1,), (1,)), ((), ())), preferred_element_type=F32)
+
+
+def dot_nn(a, b):
+    return lax.dot_general(a, b, (((1,), (0,)), ((), ())), preferred_element_type=F32)
+
+
+def polar(row):
+    value = row.astype(F32)
+    radial = jnp.floor((value + 0.5) * (1.0 / ANG))
+    return radial, value - radial * ANG
+
+
+def members(values, count):
+    ids = lax.broadcasted_iota(jnp.int32, (count, values.shape[1]), 0).astype(F32)
+    return ids == values
+
+
+def presence_kernel(bins_ref, counts_ref):
+    counts = jnp.zeros((ANG, RAD), F32)
+    for tile in range(bins_ref.shape[0]):
+        radial, angle = polar(bins_ref[tile : tile + 1, :])
+        counts += dot_nt(
+            members(angle, ANG).astype(BF16), members(radial, RAD).astype(BF16)
+        )
+    counts_ref[...] = (counts > 0.5).astype(F32)
+
+
+def below(size):
+    rows = lax.broadcasted_iota(jnp.int32, (size, size), 0)
+    cols = lax.broadcasted_iota(jnp.int32, (size, size), 1)
+    return rows, cols
+
+
+def slots_kernel(own_ref, other_ref, bins_ref, table_ref, rows_ref, span_ref):
+    present = jnp.maximum(own_ref[...], other_ref[...])
+    held = present.astype(BF16)
+    rows, cols = below(ANG)
+    within = dot_nn((cols < rows).astype(BF16), held)
+    totals = dot_nn(jnp.ones((ANG, ANG), BF16), held)
+    rows, cols = below(RAD)
+    before = dot_nn(totals.astype(BF16), (rows < cols).astype(BF16))
+    slots = within + before
+    high = jnp.floor(slots * (1.0 / 64))
+    low = slots - 64 * high
+    high = high.astype(BF16)
+    low = low.astype(BF16)
+    eye = (rows == cols).astype(BF16)
+    turned = 64 * dot_nt(eye, high) + dot_nt(eye, low)
+    table_ref[...] = jnp.where(dot_nt(eye, held) > 0.5, turned, -1.0).astype(jnp.int32)
+    for tile in range(bins_ref.shape[0]):
+        radial, angle = polar(bins_ref[tile : tile + 1, :])
+        ring = members(radial, RAD).astype(BF16)
+        value = 64 * dot_nn(high, ring) + dot_nn(low, ring)
+        value = jnp.sum(jnp.where(members(angle, ANG), value, 0.0), axis=0, keepdims=True)
+        rows_ref[tile : tile + 1, :] = value.astype(jnp.int32)
+    found = rows_ref[...]
+    first = jnp.min(found, axis=1, keepdims=True)
+    last = jnp.max(found, axis=1, keepdims=True)
+    lane = lax.broadcasted_iota(jnp.int32, (found.shape[0], 128), 1)
+    span_ref[...] = jnp.where(lane == 0, first, last)
+
+
+def binning_kernel(core_ref, span_ref, rows_ref, pixels_ref, mine_ref, theirs_ref, sums, turned):
+    sums[...] = jnp.zeros_like(sums)
+    across = 256 // 16
+
+    def one_tile(tile, _):
+        down = (tile // across) * 16
+        right = (tile % across) * 16
+        block = pixels_ref[pl.ds(down, 16), pl.ds(right, 16), :].reshape(TILE, 128)
+        row = rows_ref[pl.ds(tile, 1), :]
+        base = jnp.minimum(span_ref[tile, 0], ROOM) // 8 * 8
+        stop = jnp.minimum(span_ref[tile, 1] + 1, ROOM)
+
+        def one_window(step, _):
+            at = pl.multiple_of(base + step * WINDOW, 8)
+            ids = lax.broadcasted_iota(jnp.int32, (WINDOW, TILE), 0) + at
+            hits = (ids == row).astype(BF16)
+            sums[pl.ds(at, WINDOW), :] += dot_nn(hits, block)
+            return 0
+
+        lax.fori_loop(0, (stop - base + WINDOW - 1) // WINDOW, one_window, 0)
+        return 0
+
+    lax.fori_loop(0, rows_ref.shape[0], one_tile, 0)
+    for block in range(ROOM // 128):
+        turned[:, block * 128 : (block + 1) * 128] = sums[
+            block * 128 : (block + 1) * 128, :
+        ].T
+    core = core_ref[0]
+    half = turned.shape[0] // 2
+    mine_ref[...] = turned[pl.ds(pl.multiple_of(core * half, half), half), :]
+    theirs_ref[...] = turned[
+        pl.ds(pl.multiple_of((1 - core) * half, half), half), :
+    ].astype(BF16)
+
+
+def columns_kernel(first, count, range_ref, table_ref, templates_ref, turned_ref, out_ref):
+    rows = templates_ref.shape[0]
+    extra = turned_ref.shape[0]
+    for seg in range(count):
+        offset = 0 if first + seg < 4 else SEG
+
+        def one_window(window, _):
+            at = offset + window * 256
+
+            def one_pair(pair, total):
+                main, side = total
+                col = pl.multiple_of(pair * PAIR, 128)
+                row = table_ref[first + seg, pl.ds(pair, 1), :]
+                ids = lax.broadcasted_iota(jnp.int32, (256, PAIR), 0) + at
+                hits = (ids == row).astype(BF16)
+                main = main + dot_nt(templates_ref[:, pl.ds(col, PAIR)], hits)
+                side = side + dot_nt(turned_ref[:, pl.ds(col, PAIR)], hits)
+                return main, side
+
+            main, side = lax.fori_loop(
+                range_ref[first + seg, 2 * window],
+                range_ref[first + seg, 2 * window + 1],
+                one_pair,
+                (jnp.zeros((rows, 256), F32), jnp.zeros((extra, 256), F32)),
+            )
+            to = pl.multiple_of(window * 256, 256)
+            out_ref[seg, :rows, pl.ds(to, 256)] = main.astype(BF16)
+            out_ref[seg, rows:, pl.ds(to, 256)] = side.astype(BF16)
+            return 0
+
+        lax.fori_loop(0, SEG // 256, one_window, 0)
+
+
+def columns(first, count, ranges, tables, templates, turned):
+    height = templates.shape[0] + turned.shape[0]
+    return pl.pallas_call(
+        functools.partial(columns_kernel, first, count),
+        out_shape=jax.ShapeDtypeStruct((count, height, SEG), BF16),
+        in_specs=[smem(), vmem(), vmem(), vmem()],
+        out_specs=vmem(),
+        compiler_params=pltpu.CompilerParams(vmem_limit_bytes=48 * MIB),
+        name="columns",
+    )(ranges, tables, templates, turned)
+
+
+def squares_kernel(place_ref, base_ref, start_ref, table_ref, *refs):
+    lists, out_ref = refs[:-1], refs[-1]
+    share = table_ref.shape[1] // 4
+    total = jnp.zeros((8, 64), F32)
+
+    def one_pair(step, total):
+        pair = place_ref[0] * share + step
+        dense = jnp.zeros((64, PAIR), F32)
+        for seg in range(SEGS):
+            ref, index = lists[seg // 2], seg % 2
+            offset = 0 if seg < 4 else SEG
+            row = table_ref[seg, pl.ds(pair, 1), :]
+            width = 512
+            at = pl.multiple_of(start_ref[seg, pair], 128)
+            ids = lax.broadcasted_iota(jnp.int32, (width, PAIR), 0) + at + offset
+            hits = (ids == row).astype(BF16)
+            dense = dense + dot_nn(ref[index, :, pl.ds(at, width)], hits)
+        square = dense * dense
+        high = square.astype(BF16)
+        low = (square - high.astype(F32)).astype(BF16)
+        ones = jnp.ones((8, PAIR), BF16)
+        return total + dot_nt(ones, high) + dot_nt(ones, low)
+
+    out_ref[...] = lax.fori_loop(0, share, one_pair, total)
+
+
+def insert_sorted(best, value):
+    out = []
+    for held in best:
+        out.append(jnp.maximum(held, value))
+        value = jnp.minimum(held, value)
+    return out
+
+
+def merge_sorted(first, second):
+    count = len(first)
+    both = [jnp.maximum(first[i], second[count - 1 - i]) for i in range(count)]
+    gap = count // 2
+    while gap:
+        for i in range(count):
+            if i & gap == 0:
+                high = jnp.maximum(both[i], both[i + gap])
+                low = jnp.minimum(both[i], both[i + gap])
+                both[i], both[i + gap] = high, low
+        gap //= 2
+    return both
+
+
+def score_kernel(first, last, rows, *refs):
+    count = 0 if first else 1
+    own_ref, pair_ref, z_ref, x_ref, y_ref, d_ref, e_ref = refs[:7]
+    rest = refs[7:]
+    if not first:
+        so_far_ref, rest = rest[0], rest[1:]
+    if last:
+        local_ref, rank_ref, out_ref, total, lists = rest
+    else:
+        out_ref, lists = rest
+        total = out_ref
+    half = z_ref.shape[1]
+    for seg in range(z_ref.shape[0]):
+        lists[0:half, :] = z_ref[seg]
+        lists[half : 2 * half, :] = x_ref[seg]
+        lists[2 * half : 3 * half, :] = y_ref[seg]
+        lists[3 * half : 3 * half + half // 2, :] = d_ref[seg]
+        lists[3 * half + half // 2 :, :] = e_ref[seg]
+        for side, ref in enumerate((own_ref, pair_ref)):
+            term = dot_nt(ref[seg], lists[...])
+            if seg == 0 and first:
+                total[side] = term
+            elif seg == 0:
+                total[side] = so_far_ref[side] + term
+            else:
+                total[side] = total[side] + term
+    if not last:
+        return
+    width = total.shape[2]
+    low = jnp.full((8, width), -jnp.inf, F32)
+    best = [low] * TOPK
+    for side in range(2):
+        def step(at, best):
+            return tuple(
+                insert_sorted(best, total[side, pl.ds(pl.multiple_of(at * 8, 8), 8), :])
+            )
+
+        best = lax.fori_loop(0, rows // 8, step, tuple(best), unroll=2)
+    for turn in (4, 2, 1):
+        best = merge_sorted(best, [pltpu.roll(part, turn, 0) for part in best])
+    for place in range(TOPK):
+        out_ref[place : place + 1, :] = best[place][0:1, :]
+    picked = [jnp.zeros((1, width), F32) for _ in range(3)]
+    for side in range(2):
+        ids = lax.broadcasted_iota(jnp.int32, (rows, width), 0)
+        picked[1] += jnp.sum(
+            jnp.where(ids == local_ref[side : side + 1, :], total[side, :rows, :], 0.0),
+            axis=0,
+            keepdims=True,
+        )
+        ids = lax.broadcasted_iota(jnp.int32, (KEPT, width), 0)
+        hit = ids == rank_ref[side : side + 1, :]
+        picked[0] += jnp.sum(
+            jnp.where(hit, total[side, rows : rows + KEPT, :], 0.0), axis=0, keepdims=True
+        )
+        picked[2] += jnp.sum(
+            jnp.where(hit, total[side, rows + KEPT :, :], 0.0), axis=0, keepdims=True
+        )
+    for place in range(3):
+        out_ref[TOPK + place : TOPK + place + 1, :] = picked[place]
+    out_ref[TOPK + 3 :, :] = jnp.zeros((16 - TOPK - 3, width), F32)
+
+
+def score(first, last, rows, own, pair, lists, so_far, extra):
+    height = own.shape[1]
+    width = 4 * lists[0].shape[1]
+    scratch = [pltpu.VMEM((width, SEG), BF16)]
+    if last:
+        scratch = [pltpu.VMEM((2, height, width), F32)] + scratch
+        shape = (16, width)
+    else:
+        shape = (2, height, width)
+    args = [own, pair, *lists]
+    if not first:
+        args.append(so_far)
+    args.extend(extra)
+    return pl.pallas_call(
+        functools.partial(score_kernel, first, last, rows),
+        out_shape=jax.ShapeDtypeStruct(shape, F32),
+        in_specs=[vmem()] * len(args),
+        out_specs=vmem(),
+        scratch_shapes=scratch,
+        compiler_params=pltpu.CompilerParams(vmem_limit_bytes=48 * MIB),
+        name="score",
+    )(*args)
+
+
+def merge_kernel(scale, *refs):
+    parts, out_ref = refs[:-1], refs[-1]
+    best = None
+    for ref in parts:
+        rows = [ref[place : place + 1, :] for place in range(TOPK)]
+        best = rows if best is None else merge_sorted(best, rows)
+    rest = (parts[0][TOPK:, :] + parts[2][TOPK:, :]) + (
+        parts[1][TOPK:, :] + parts[3][TOPK:, :]
+    )
+    factor = lax.rsqrt(rest[3:4, :] / BINS + EPS) if scale else 1.0
+    for place in range(TOPK):
+        out_ref[place : place + 1, :] = best[place] * factor
+    out_ref[TOPK:, :] = rest * factor
+
+
+def merge(scale, parts):
+    return pl.pallas_call(
+        functools.partial(merge_kernel, scale),
+        out_shape=jax.ShapeDtypeStruct(parts[0].shape, F32),
+        in_specs=[vmem()] * len(parts),
+        out_specs=vmem(),
+        name="merge",
+    )(*parts)
+
+
+def compact_body(patterns, detector_gain, background, bin_map, templates, best_picks):
+    orients = lax.axis_size("orient")
+    chips = orients // 2
+    section = lax.axis_index("section")
+    orient = lax.axis_index("orient")
+    core = orient % 2
+    chip = orient // 2
+    rows = templates.shape[0]
+    count = patterns.shape[1]
+    half = count // 2
+    pixels = patterns.shape[2]
+
+    def swap(x):
+        return lax.ppermute(x, "orient", [(i, i ^ 1) for i in range(orients)])
+
+    def along(x, by):
+        return lax.ppermute(x, "orient", [(i, (i + 2 * by) % orients) for i in range(orients)])
+
+    def hops(x, pairs):
+        return lax.ppermute(
+            x, "orient", [(2 * i + c, 2 * j + c) for i, j in pairs for c in range(2)]
+        )
+
+    def across(x, by):
+        return lax.ppermute(x, "section", [(i, i ^ by) for i in range(4)])
+
+    tiles = pixels // TILE
+    bins = bin_map.reshape(tiles // 16, 16, 16, 16).transpose(0, 2, 1, 3).reshape(tiles, TILE)
+    present = pl.pallas_call(
+        presence_kernel,
+        out_shape=jax.ShapeDtypeStruct((ANG, RAD), F32),
+        in_specs=[vmem()],
+        out_specs=vmem(),
+        name="presence",
+    )(bins)
+    other = swap(present)
+    corrected = ((patterns[0].astype(F32) - background) * detector_gain).astype(BF16)
+    corrected = corrected.T.reshape(tiles, TILE, count)
+    table, slot_rows, span = pl.pallas_call(
+        slots_kernel,
+        out_shape=(
+            jax.ShapeDtypeStruct((RAD, ANG), jnp.int32),
+            jax.ShapeDtypeStruct((tiles, TILE), jnp.int32),
+            jax.ShapeDtypeStruct((tiles, 128), jnp.int32),
+        ),
+        in_specs=[vmem()] * 3,
+        out_specs=(vmem(),) * 3,
+        name="slots",
+    )(present, other, bins)
+    mine, theirs = pl.pallas_call(
+        binning_kernel,
+        out_shape=(
+            jax.ShapeDtypeStruct((half, ROOM), F32),
+            jax.ShapeDtypeStruct((half, ROOM), BF16),
+        ),
+        in_specs=[smem(), smem(), vmem(), vmem()],
+        out_specs=(vmem(), vmem()),
+        scratch_shapes=[pltpu.VMEM((ROOM + WINDOW, count), F32), pltpu.VMEM((count, ROOM), F32)],
+        compiler_params=pltpu.CompilerParams(vmem_limit_bytes=24 * MIB),
+        name="binning",
+    )(core.reshape(1).astype(jnp.int32), span, slot_rows, corrected)
+    received = swap(theirs)
+    summed = (mine + received.astype(F32)).astype(BF16)
+    base = summed[:, :SEG]
+    spare = summed[:, SEG:]
+
+    table = table.reshape(RAD // 2, PAIR)
+    tables = jnp.stack([table] + [along(table, by) for by in range(1, chips)])
+    near = jnp.where(chip < 2, (chip - 1) % chips, (chip - 2) % chips)
+    far = jnp.where(chip < 2, (chip - 2) % chips, (chip - 1) % chips)
+    tables = jnp.concatenate(
+        [
+            tables,
+            lax.dynamic_index_in_dim(tables, near, 0),
+            lax.dynamic_index_in_dim(tables, far, 0),
+        ]
+    )
+    valid = jnp.sum((tables >= 0).astype(jnp.int32), axis=2)
+    ends = jnp.cumsum(valid, axis=1)
+    begins = ends - valid
+    offsets = jnp.array([0] * 4 + [SEG] * 2, jnp.int32)
+    at = offsets[:, None] + 256 * lax.iota(jnp.int32, SEG // 256)[None, :]
+    low = jnp.sum((ends[:, None, :] <= at[:, :, None]).astype(jnp.int32), axis=2)
+    high = jnp.sum((begins[:, None, :] < at[:, :, None] + 256).astype(jnp.int32), axis=2)
+    ranges = jnp.stack([low, high], axis=2).reshape(SEGS, -1)
+    starts = jnp.clip((begins - offsets[:, None]) // 128 * 128, 0, SEG - 512)
+    held_chip = (chip - lax.iota(jnp.int32, chips)) % chips
+    room = jnp.where((held_chip == 1) | (held_chip == 2), ROOM, SEG)
+    crowded = jnp.any(ends[:chips, -1] > room)
+
+    picks = best_picks.reshape(-1)
+    owner = picks // rows
+    ids = lax.iota(jnp.int32, picks.shape[0])
+    earlier = ids[:, None] < ids[None, :]
+    first = ~jnp.any(earlier & (picks[:, None] == picks[None, :]), axis=0)
+    rank = jnp.sum(
+        (earlier & first[:, None] & (owner[:, None] == owner[None, :])).astype(jnp.int32), axis=0
+    )
+    crowded = crowded | jnp.any(first & (rank >= KEPT))
+    me = section * orients + orient
+    chosen = first & (owner == me)
+    wanted = jnp.sum(
+        jnp.where(
+            chosen[None, :] & (rank[None, :] == lax.iota(jnp.int32, KEPT)[:, None]),
+            (picks - me * rows)[None, :] + 1,
+            0,
+        ),
+        axis=1,
+    )
+    select = (wanted[:, None] - 1 == lax.iota(jnp.int32, rows)[None, :]).astype(BF16)
+    taken = lax.dot_general(
+        select, templates, (((1,), (0,)), ((), ())), preferred_element_type=BF16
+    ).reshape(KEPT, RAD, ANG)
+    turned = jnp.concatenate([jnp.roll(taken, 1, axis=2), jnp.roll(taken, -1, axis=2)])
+    turned = turned.reshape(2 * KEPT, BINS)
+    first_rank = jnp.sum(
+        jnp.where(first[:, None] & (picks[:, None] == picks[None, :]), rank[:, None], 0), axis=0
+    )
+    order = [section ^ by for by in range(4)]
+
+    def arranged(values):
+        values = values.reshape(best_picks.shape)
+        return jnp.concatenate(
+            [lax.dynamic_slice(values, (s, core * half), (1, half))[0] for s in order]
+        )
+
+    picks_here = arranged(picks)
+    rank_here = arranged(first_rank)
+    bases = jnp.stack([me * rows, (section * orients + (orient ^ 1)) * rows])
+    local = picks_here[None, :] - bases[:, None]
+    held = (local >= 0) & (local < rows)
+    local = jnp.where(held, local, -1)
+    ranks = jnp.where(held, rank_here[None, :], -1)
+
+    bases_z = [base] + [along(base, by) for by in range(1, chips)]
+    step = hops(spare, [(1, 0), (2, 3)])
+    inner = (chip == 1) | (chip == 2)
+    traded = hops(spare, [(1, 2), (2, 1)])
+    far_part = hops(spare, [(1, 3), (2, 0)])
+    spare_near = jnp.where(inner, spare, step)
+    spare_far = jnp.where(inner, traded, far_part)
+    groups = [
+        jnp.stack([bases_z[0], bases_z[1]]),
+        jnp.stack([bases_z[2], bases_z[3]]),
+        jnp.stack([spare_near, spare_far]),
+    ]
+    lists = []
+    for group in groups:
+        x = across(group, 1)
+        y = across(group, 2)
+        d = across(x[:, : half // 2], 2)
+        e = across(y[:, half // 2 :], 1)
+        lists.append((group, x, y, d, e))
+
+    own = [columns(2 * i, 2, ranges, tables, templates, turned) for i in range(3)]
+    pair = [swap(part) for part in own]
+    squares = pl.pallas_call(
+        squares_kernel,
+        out_shape=jax.ShapeDtypeStruct((8, half), F32),
+        in_specs=[smem(), smem(), smem(), vmem()] + [vmem()] * 3,
+        out_specs=vmem(),
+        name="squares",
+    )(
+        chip.reshape(1).astype(jnp.int32),
+        offsets,
+        starts,
+        tables,
+        *groups,
+    )
+    total = score(True, False, rows, own[0], pair[0], lists[0], None, ())
+    total = score(False, False, rows, own[1], pair[1], lists[1], total, ())
+    pack = score(False, True, rows, own[2], pair[2], lists[2], total, (local, ranks))
+    parts = [pack[:, :half]]
+    for by in range(1, 4):
+        parts.append(across(pack[:, by * half : (by + 1) * half], by))
+    part = merge(False, parts)
+    part = lax.dynamic_update_slice(part, squares[:1], (TOPK + 3, 0))
+    part = merge(True, [part] + [along(part, by) for by in range(1, chips)])
+    partner = swap(part)
+    both = jnp.where(
+        core == 0,
+        jnp.concatenate([part, partner], axis=1),
+        jnp.concatenate([partner, part], axis=1),
+    ).T
+    mine_rows = lax.dynamic_slice(both, (orient * (count // orients), TOPK), (count // orients, 3))
+    sparse = (both[None, :, :TOPK], mine_rows[None])
+    return lax.cond(
+        crowded,
+        lambda: dense_body(
+            patterns, detector_gain, background, bin_map, templates, best_picks
+        ),
+        lambda: sparse,
+    )
+
+
 def solution(mesh):
+    sizes = dict(mesh.shape)
+    fits = sizes["section"] == 4 and sizes["orient"] == 8
     return jax.shard_map(
-        body,
+        compact_body if fits else dense_body,
         mesh=mesh,
         in_specs=(
             P("section", None, "orient"),

time: 596 us -> 280 us (0.47); the launches traced: 587 us -> 278 us
  local copies, waits for them, and re-layouts: 175 us -> 29 us
  other arithmetic: 147 us -> 12.3 us
  Pallas kernels: 0 us -> 115 us
  matrix products: 107 us -> 5.56 us
  waiting for transfers between devices: 120 us -> 49.7 us
  starting transfers between devices: 9.06 us -> 50.7 us
  blocking collectives: 14 us -> 0 us
    pallas_call x0 -> x12, Pallas kernels: none -> 115 us  [the longest x3 69.9 us: columns(): pl.pallas_call(functools.partial(columns_kernel, first, count), out_shape...]
    dot_general x32 -> x1, matrix products: 82.4 us -> 5.56 us  [compact_body(): lax.dot_general(select, templates, (((1,), (0,)), ((), ())), preferred_el...]
    ppermute x7 -> x33, waiting for transfers between devices: 103 us -> 49.7 us  [the longest x15 25.9 us: across(): return lax.ppermute(x, 'section', [(i, i ^ by) for i in range(4)])]
    convert_element_type x8 -> x0, local copies, waits for them, and re-layouts: 53 us -> none  [score_batch(): rolled.astype(jnp.float32)]
    gather x4 -> x0, local copies, waits for them, and re-layouts: 41.8 us -> none  [score_batch(): chosen = jnp.take(templates, jnp.clip(local, 0, count - 1), axis=0)]
    ppermute x7 -> x33, starting transfers between devices: 8.98 us -> 50.7 us  [the longest x9 25.4 us: along(): lax.ppermute(x, 'orient', [(i, (i + 2 * by) % orients) for i in range(ori...]
    top_k x14 -> x0, other arithmetic: 37.7 us -> none  [the longest x4 30.5 us: score_batch(): best = lax.top_k(scores, TOPK)[0]]
    reduce_sum x5, other arithmetic: 33.8 us -> 1.78 us  [the longest x1 0.92 us: compact_body(): jnp.sum(jnp.where(first[:, None] & (picks[:, None] == picks[None, :]), ra...]
  transfers between devices with their start and end apart: 9 -> 33, of which waited for: 6 -> 15; matrix products, arithmetic and copies ran while one was open for 39% -> 11% of each run, Pallas kernels for 0% -> 36%
where the time goes in v1:
time: 280 us; the launch traced here: 278 us
  Pallas kernels  115 us (41%)
  starting transfers between devices  50.7 us (18%)
  waiting for transfers between devices  49.7 us (18%)
  local copies, waits for them, and re-layouts  29 us (10%)
  between operations  15.9 us (6%)
  other arithmetic  12.3 us (4%)
  matrix products  5.56 us (2%)
    pallas_call x3, Pallas kernels, columns(): pl.pallas_call(functools.partial(columns_kernel, first, count), out_shape...  69.9 us
    ppermute x15, waiting for transfers between devices, across(): return lax.ppermute(x, 'section', [(i, i ^ by) for i in range(4)])  25.9 us
    ppermute x9, starting transfers between devices, along(): lax.ppermute(x, 'orient', [(i, (i + 2 * by) % orients) for i in range(ori...  25.4 us
    ppermute x15, starting transfers between devices, across(): return lax.ppermute(x, 'section', [(i, i ^ by) for i in range(4)])  20 us
    pallas_call x3, Pallas kernels, score(): pl.pallas_call(functools.partial(score_kernel, first, last, rows), out_sh...  15.7 us
    ppermute x9, waiting for transfers between devices, along(): lax.ppermute(x, 'orient', [(i, (i + 2 * by) % orients) for i in range(ori...  14.5 us
    pallas_call x1, Pallas kernels, compact_body(): pl.pallas_call(binning_kernel, out_shape=(jax.ShapeDtypeStruct((half, ROO...  12.2 us
    ppermute x3, waiting for transfers between devices, hops(): lax.ppermute(x, 'orient', [(2 * i + c, 2 * j + c) for i, j in pairs for c...  9.22 us
  transfers between devices with their start and end apart: 33, of which 15 were waited for; matrix products, arithmetic and copies ran while one was open for 11% of the time, Pallas kernels for 36%

profile of v1, /device:TPU:0, one launch (start us, length us, event | category | flops | bytes accessed | tf_op | source)
XLA Modules:
  0.0 278.2 jit_solution(1018241822340788161)
XLA Ops:
  14.4 5.6 %fusion.35 = bf16[32,12288]{1,0:T(8,128)(2,1)S(1)} fusion(bf16[400,12288]{1,0:T(8,128)(2,1)} %templates_ref.5, s32[32]{0:T(128)S(1)} %broadcast_add_fusion.2), kind=kOutput, calls=%fused_computation.127 | convolution fusion | flops 314585600 | bytes 10616960 | tf_op jit(solution)/shard_map/dot_general | solution.py:546
  25.5 2.5 copy.117
  28.0 3.5 %reshape.313.turned_ref = bf16[64,12288]{1,0:T(8,128)(2,1)S(1)} reshape(bf16[64,64,192]{2,1,0:T(8,128)(2,1)} %maximum_maximum_fusion) | data formatting | bytes 3145728 | tf_op jit(solution)/shard_map/reshape | solution.py:550
  32.2 3.9 %slots.1 = (s32[64,192]{1,0:T(8,128)}, s32[32,256]{1,0:T(8,128)}, s32[32,128]{1,0:T(8,128)}) custom-call(f32[192,64]{1,0:T(8,128)} %presence.1.own_ref, f32[192,64]{1,0:T(8,128)} %copy-done.34, s32[32,256]{1,0:T(8,128)} %reshape.309.bins_ref), custom_call_target="tpu_custom_call" | custom-call | tf_op jit(solution)/shard_map/slots/pallas_call | solution.py:474
  37.6 2.6 collective-permute-start.8
  40.2 2.6 collective-permute-start.9
  48.1 12.2 %binning.1 = (f32[64,3584]{1,0:T(8,128)S(1)}, bf16[64,3584]{1,0:T(8,128)(2,1)S(1)}) custom-call(s32[1]{0:T(128)} %bitcast.49.core_ref, s32[32,128]{1,0:T(8,128)S(1)} %copy-done.8, s32[32,256]{1,0:T(8,128)S(1)} %copy-done.7, bf16[32,256,128]{2,1,0:T(8,128)(2,1)S(1)} %bitcast.189), custom_call_target="tpu_custom_call" | custom-call | tf_op jit(solution)/shard_map/binning/pallas_call | solution.py:485
  65.2 25.8 %columns.5.refs_0_ = bf16[2,464,1792]{2,1,0:T(8,128)(2,1)} custom-call(s32[6,14]{1,0:T(8,128)S(1)} %copy.116.range_ref, s32[6,32,384]{2,1,0:T(8,128)S(1)} %dynamic-slice_dynamic-update-slice_fusion.table_ref, bf16[400,12288]{1,0:T(8,128)(2,1)} %templates_ref.5, bf16[64,12288]{1,0:T(8,128)(2,1)S(1)} %reshape.313.turned_ref), custom_call_target="tpu_custom_call" | custom-call | tf_op jit(solution)/shard_map/columns/pallas_call | solution.py:266
  91.3 19.1 %columns.4.refs_0_ = bf16[2,464,1792]{2,1,0:T(8,128)(2,1)} custom-call(s32[6,14]{1,0:T(8,128)S(1)} %copy.116.range_ref, s32[6,32,384]{2,1,0:T(8,128)S(1)} %dynamic-slice_dynamic-update-slice_fusion.table_ref, bf16[400,12288]{1,0:T(8,128)(2,1)} %templates_ref.5, bf16[64,12288]{1,0:T(8,128)(2,1)S(1)} %reshape.313.turned_ref), custom_call_target="tpu_custom_call" | custom-call | tf_op jit(solution)/shard_map/columns/pallas_call | solution.py:266
  110.5 25.0 %columns.3.refs_0_ = bf16[2,464,1792]{2,1,0:T(8,128)(2,1)} custom-call(s32[6,14]{1,0:T(8,128)S(1)} %copy.116.range_ref, s32[6,32,384]{2,1,0:T(8,128)S(1)} %dynamic-slice_dynamic-update-slice_fusion.table_ref, bf16[400,12288]{1,0:T(8,128)(2,1)} %templates_ref.5, bf16[64,12288]{1,0:T(8,128)(2,1)S(1)} %reshape.313.turned_ref), custom_call_target="tpu_custom_call" | custom-call | tf_op jit(solution)/shard_map/columns/pallas_call | solution.py:266
  138.0 15.1 %collective-permute-start.28 = (bf16[64,1792]{1,0:T(8,128)(2,1)S(1)}, bf16[64,1792]{1,0:T(8,128)(2,1)S(1)}, u32[]{:S(2)}, u32[]{:S(2)}) collective-permute-start(bf16[64,1792]{1,0:T(8,128)(2,1)S(1)} %get-tuple-element.273), channel_id=1, source_target_pairs={{0,2},{1,3},{2,4},{3,5},{4,6},{5,7},{6,0},{7,1},{8,10},{9,11},{10,... | collective-permute-start | bytes 688136 | tf_op jit(solution)/shard_map/ppermute | solution.py:452
  153.1 9.2 %collective-permute-done.15 = bf16[64,1792]{1,0:T(8,128)(2,1)S(1)} collective-permute-done((bf16[64,1792]{1,0:T(8,128)(2,1)S(1)}, bf16[64,1792]{1,0:T(8,128)(2,1)S(1)}, u32[]{:S(2)}, u32[]{:S(2)}) %collective-permute-start.15) | collective-permute-done | bytes 229408 | tf_op jit(solution)/shard_map/ppermute | solution.py:455
  162.5 9.2 %collective-permute-done.21 = bf16[64,1792]{1,0:T(8,128)(2,1)S(1)} collective-permute-done((bf16[64,1792]{1,0:T(8,128)(2,1)S(1)}, bf16[64,1792]{1,0:T(8,128)(2,1)S(1)}, u32[]{:S(2)}, u32[]{:S(2)}) %collective-permute-start.21) | collective-permute-done | bytes 229408 | tf_op jit(solution)/shard_map/ppermute | solution.py:452
  176.5 6.0 %collective-permute-done.16.refs_3_ = bf16[2,64,1792]{2,1,0:T(8,128)(2,1)S(1)} collective-permute-done((bf16[2,64,1792]{2,1,0:T(8,128)(2,1)S(1)}, bf16[2,64,1792]{2,1,0:T(8,128)(2,1)S(1)}, u32[]{:S(2)}, u32[]{:S(2)}) %collective-permute-start.16) | collective-permute-done | bytes 458784 | tf_op jit(solution)/shard_map/ppermute | solution.py:460
  183.9 2.6 collective-permute-done.17.refs_4_
  188.1 5.0 %collective-permute-done.29.refs_3_ = bf16[2,64,1792]{2,1,0:T(8,128)(2,1)S(1)} collective-permute-done((bf16[2,64,1792]{2,1,0:T(8,128)(2,1)S(1)}, bf16[2,64,1792]{2,1,0:T(8,128)(2,1)S(1)}, u32[]{:S(2)}, u32[]{:S(2)}) %collective-permute-start.29) | collective-permute-done | bytes 458784 | tf_op jit(solution)/shard_map/ppermute | solution.py:460
  194.6 2.6 collective-permute-done.30.refs_4_
  199.5 2.6 collective-permute-done.23.refs_3_
  206.9 2.7 collective-permute-done.24.refs_4_
  217.5 2.5 collective-permute-done.25.refs_5_
  223.2 4.9 %score.3.refs_7_ = f32[2,464,256]{2,1,0:T(8,128)S(1)} custom-call(bf16[2,464,1792]{2,1,0:T(8,128)(2,1)} %columns.5.refs_0_, bf16[2,464,1792]{2,1,0:T(8,128)(2,1)} %collective-permute-done.27.refs_1_, bf16[2,64,1792]{2,1,0:T(8,128)(2,1)S(1)} %pad_maximum_fusion.18.refs_2_.refs_0_, bf16[2,64,1792]{2,1,0:T(8,128)(2,1)S(1)} %collective-permute-done.29.refs_3_, ...), custom_call_target="tpu_custom_call" | custom-call | tf_op jit(solution)/shard_map/score/pallas_call | solution.py:400
  228.5 4.9 %score.4.refs_7_ = f32[2,464,256]{2,1,0:T(8,128)S(1)} custom-call(bf16[2,464,1792]{2,1,0:T(8,128)(2,1)} %columns.4.refs_0_, bf16[2,464,1792]{2,1,0:T(8,128)(2,1)} %collective-permute-done.20.refs_1_, bf16[2,64,1792]{2,1,0:T(8,128)(2,1)S(1)} %pad_maximum_fusion.17.refs_2_.refs_1_, bf16[2,64,1792]{2,1,0:T(8,128)(2,1)S(1)} %collective-permute-done.23.refs_3_, ...), custom_call_target="tpu_custom_call" | custom-call | tf_op jit(solution)/shard_map/score/pallas_call | solution.py:400
  233.5 5.9 %score.5 = f32[16,256]{1,0:T(8,128)S(1)} custom-call(bf16[2,464,1792]{2,1,0:T(8,128)(2,1)} %columns.3.refs_0_, bf16[2,464,1792]{2,1,0:T(8,128)(2,1)} %collective-permute-done.11.refs_1_, bf16[2,64,1792]{2,1,0:T(8,128)(2,1)S(1)} %pad_maximum_fusion.16.refs_2_, bf16[2,64,1792]{2,1,0:T(8,128)(2,1)S(1)} %collective-permute-done.16.refs_3_, ...), custom_call_target="tpu_custom_call" | custom-call | tf_op jit(solution)/shard_map/score/pallas_call | solution.py:400
  244.2 8.3 %squares.1 = f32[8,64]{1,0:T(8,128)} custom-call(s32[1]{0:T(128)} %bitcast.70.place_ref, s32[6]{0:T(128)} %constant.312.clone.base_ref, s32[6,32]{1,0:T(8,128)} %get-tuple-element.233.start_ref, s32[6,32,384]{2,1,0:T(8,128)} %copy-done.1, bf16[2,64,1792]{2,1,0:T(8,128)(2,1)} %copy-done.3, bf16[2,64,1792]{2,1,0:T(8,128)(2,1)} %copy-done.4, ...), custom_call_target="tpu_custom_call" | custom-call | tf_op jit(solution)/shard_map/squares/pallas_call | solution.py:592
  (168 shorter events, 78.6 us)
Async XLA Ops:
  11.3 20.3 %collective-permute-start.7 = (f32[192,64]{1,0:T(8,128)}, f32[192,64]{1,0:T(8,128)S(1)}, u32[]{:S(2)}, u32[]{:S(2)}) collective-permute-start(f32[192,64]{1,0:T(8,128)} %presence.1.own_ref), channel_id=1, source_target_pairs={{0,1},{1,0},{2,3},{3,2},{4,5},{5,4},{6,7},{7,6},{8,9},{9,8},{10,11... | collective-permute-start | bytes 147464 | tf_op jit(solution)/shard_map/ppermute | solution.py:449
  37.6 23.2 %collective-permute-start.8 = (s32[32,384]{1,0:T(8,128)}, s32[32,384]{1,0:T(8,128)S(1)}, u32[]{:S(2)}, u32[]{:S(2)}) collective-permute-start(s32[32,384]{1,0:T(8,128)} %reshape.310), channel_id=1, source_target_pairs={{0,2},{1,3},{2,4},{3,5},{4,6},{5,7},{6,0},{7,1},{8,10},{9,11},{10,... | collective-permute-start | bytes 147464 | tf_op jit(solution)/shard_map/ppermute | solution.py:452
  40.2 20.6 %collective-permute-start.9 = (s32[32,384]{1,0:T(8,128)}, s32[32,384]{1,0:T(8,128)S(1)}, u32[]{:S(2)}, u32[]{:S(2)}) collective-permute-start(s32[32,384]{1,0:T(8,128)} %reshape.310), channel_id=1, source_target_pairs={{0,4},{1,5},{2,6},{3,7},{4,0},{5,1},{6,2},{7,3},{8,12},{9,13},{10,... | collective-permute-start | bytes 147464 | tf_op jit(solution)/shard_map/ppermute | solution.py:452
  42.8 18.0 %collective-permute-start.10 = (s32[32,384]{1,0:T(8,128)}, s32[32,384]{1,0:T(8,128)S(1)}, u32[]{:S(2)}, u32[]{:S(2)}) collective-permute-start(s32[32,384]{1,0:T(8,128)} %reshape.310), channel_id=1, source_target_pairs={{0,6},{1,7},{2,0},{3,1},{4,2},{5,3},{6,4},{7,5},{8,14},{9,15},{10,... | collective-permute-start | bytes 147464 | tf_op jit(solution)/shard_map/ppermute | solution.py:452
  63.5 73.2 %collective-permute-start.13 = (bf16[64,1792]{1,0:T(8,128)(2,1)S(1)}, bf16[64,1792]{1,0:T(8,128)(2,1)S(1)}, u32[]{:S(2)}, u32[]{:S(2)}) collective-permute-start(bf16[64,1792]{1,0:T(8,128)(2,1)S(1)} %slice.210), channel_id=1, source_target_pairs={{2,0},{3,1},{4,6},{5,7},{10,8},{11,9},{12,14},{13,15},{18,16},{19,... | collective-permute-start | bytes 688136 | tf_op jit(solution)/shard_map/ppermute | solution.py:455
  91.0 130.5 %collective-permute-start.27 = (bf16[2,464,1792]{2,1,0:T(8,128)(2,1)}, bf16[2,464,1792]{2,1,0:T(8,128)(2,1)}, u32[]{:S(2)}, u32[]{:S(2)}) collective-permute-start(bf16[2,464,1792]{2,1,0:T(8,128)(2,1)} %columns.5.refs_0_), channel_id=1, source_target_pairs={{0,1},{1,0},{2,3},{3,2},{4,5},{5,4},{6,7},{7,6},{8,9},{9,8},{10,11... | collective-permute-start | bytes 9977864 | tf_op jit(solution)/shard_map/ppermute | solution.py:449
  135.5 93.0 %collective-permute-start.20 = (bf16[2,464,1792]{2,1,0:T(8,128)(2,1)}, bf16[2,464,1792]{2,1,0:T(8,128)(2,1)}, u32[]{:S(2)}, u32[]{:S(2)}) collective-permute-start(bf16[2,464,1792]{2,1,0:T(8,128)(2,1)} %columns.4.refs_0_), channel_id=1, source_target_pairs={{0,1},{1,0},{2,3},{3,2},{4,5},{5,4},{6,7},{7,6},{8,9},{9,8},{10,11... | collective-permute-start | bytes 9977864 | tf_op jit(solution)/shard_map/ppermute | solution.py:449
  135.6 97.8 %collective-permute-start.11 = (bf16[2,464,1792]{2,1,0:T(8,128)(2,1)}, bf16[2,464,1792]{2,1,0:T(8,128)(2,1)}, u32[]{:S(2)}, u32[]{:S(2)}) collective-permute-start(bf16[2,464,1792]{2,1,0:T(8,128)(2,1)} %columns.3.refs_0_), channel_id=1, source_target_pairs={{0,1},{1,0},{2,3},{3,2},{4,5},{5,4},{6,7},{7,6},{8,9},{9,8},{10,11... | collective-permute-start | bytes 9977864 | tf_op jit(solution)/shard_map/ppermute | solution.py:449
  136.7 25.6 %collective-permute-start.15 = (bf16[64,1792]{1,0:T(8,128)(2,1)S(1)}, bf16[64,1792]{1,0:T(8,128)(2,1)S(1)}, u32[]{:S(2)}, u32[]{:S(2)}) collective-permute-start(bf16[64,1792]{1,0:T(8,128)(2,1)S(1)} %slice.210), channel_id=1, source_target_pairs={{2,6},{3,7},{4,0},{5,1},{10,14},{11,15},{12,8},{13,9},{18,22},{19,... | collective-permute-start | bytes 688136 | tf_op jit(solution)/shard_map/ppermute | solution.py:455
  138.0 24.3 %collective-permute-start.28 = (bf16[64,1792]{1,0:T(8,128)(2,1)S(1)}, bf16[64,1792]{1,0:T(8,128)(2,1)S(1)}, u32[]{:S(2)}, u32[]{:S(2)}) collective-permute-start(bf16[64,1792]{1,0:T(8,128)(2,1)S(1)} %get-tuple-element.273), channel_id=1, source_target_pairs={{0,2},{1,3},{2,4},{3,5},{4,6},{5,7},{6,0},{7,1},{8,10},{9,11},{10,... | collective-permute-start | bytes 688136 | tf_op jit(solution)/shard_map/ppermute | solution.py:452
  162.3 9.4 %collective-permute-start.21 = (bf16[64,1792]{1,0:T(8,128)(2,1)S(1)}, bf16[64,1792]{1,0:T(8,128)(2,1)S(1)}, u32[]{:S(2)}, u32[]{:S(2)}) collective-permute-start(bf16[64,1792]{1,0:T(8,128)(2,1)S(1)} %get-tuple-element.273), channel_id=1, source_target_pairs={{0,4},{1,5},{2,6},{3,7},{4,0},{5,1},{6,2},{7,3},{8,12},{9,13},{10,... | collective-permute-start | bytes 688136 | tf_op jit(solution)/shard_map/ppermute | solution.py:452
  162.3 12.5 %collective-permute-start.22 = (bf16[64,1792]{1,0:T(8,128)(2,1)S(1)}, bf16[64,1792]{1,0:T(8,128)(2,1)S(1)}, u32[]{:S(2)}, u32[]{:S(2)}) collective-permute-start(bf16[64,1792]{1,0:T(8,128)(2,1)S(1)} %get-tuple-element.273), channel_id=1, source_target_pairs={{0,6},{1,7},{2,0},{3,1},{4,2},{5,3},{6,4},{7,5},{8,14},{9,15},{10,... | collective-permute-start | bytes 688136 | tf_op jit(solution)/shard_map/ppermute | solution.py:452
  171.7 10.7 %collective-permute-start.16 = (bf16[2,64,1792]{2,1,0:T(8,128)(2,1)S(1)}, bf16[2,64,1792]{2,1,0:T(8,128)(2,1)S(1)}, u32[]{:S(2)}, u32[]{:S(2)}) collective-permute-start(bf16[2,64,1792]{2,1,0:T(8,128)(2,1)S(1)} %pad_maximum_fusion.16.refs_2_), channel_id=1, source_target_pairs={{0,8},{8,0},{16,24},{24,16},{1,9},{9,1},{17,25},{25,17},{2,10},{10... | collective-permute-start | bytes 1376264 | tf_op jit(solution)/shard_map/ppermute | solution.py:460
  174.9 11.7 %collective-permute-start.17 = (bf16[2,64,1792]{2,1,0:T(8,128)(2,1)S(1)}, bf16[2,64,1792]{2,1,0:T(8,128)(2,1)S(1)}, u32[]{:S(2)}, u32[]{:S(2)}) collective-permute-start(bf16[2,64,1792]{2,1,0:T(8,128)(2,1)S(1)} %pad_maximum_fusion.16.refs_2_), channel_id=1, source_target_pairs={{0,16},{8,24},{16,0},{24,8},{1,17},{9,25},{17,1},{25,9},{2,18},{10... | collective-permute-start | bytes 1376264 | tf_op jit(solution)/shard_map/ppermute | solution.py:460
  182.5 10.7 %collective-permute-start.29 = (bf16[2,64,1792]{2,1,0:T(8,128)(2,1)S(1)}, bf16[2,64,1792]{2,1,0:T(8,128)(2,1)S(1)}, u32[]{:S(2)}, u32[]{:S(2)}) collective-permute-start(bf16[2,64,1792]{2,1,0:T(8,128)(2,1)S(1)} %pad_maximum_fusion.18.refs_2_.refs_0_), channel_id=1, source_target_pairs={{0,8},{8,0},{16,24},{24,16},{1,9},{9,1},{17,25},{25,17},{2,10},{10... | collective-permute-start | bytes 1376264 | tf_op jit(solution)/shard_map/ppermute | solution.py:460
  186.5 10.7 %collective-permute-start.30 = (bf16[2,64,1792]{2,1,0:T(8,128)(2,1)S(1)}, bf16[2,64,1792]{2,1,0:T(8,128)(2,1)S(1)}, u32[]{:S(2)}, u32[]{:S(2)}) collective-permute-start(bf16[2,64,1792]{2,1,0:T(8,128)(2,1)S(1)} %pad_maximum_fusion.18.refs_2_.refs_0_), channel_id=1, source_target_pairs={{0,16},{8,24},{16,0},{24,8},{1,17},{9,25},{17,1},{25,9},{2,18},{10... | collective-permute-start | bytes 1376264 | tf_op jit(solution)/shard_map/ppermute | solution.py:460
  193.1 9.0 %collective-permute-start.23 = (bf16[2,64,1792]{2,1,0:T(8,128)(2,1)S(1)}, bf16[2,64,1792]{2,1,0:T(8,128)(2,1)S(1)}, u32[]{:S(2)}, u32[]{:S(2)}) collective-permute-start(bf16[2,64,1792]{2,1,0:T(8,128)(2,1)S(1)} %pad_maximum_fusion.17.refs_2_.refs_1_), channel_id=1, source_target_pairs={{0,8},{8,0},{16,24},{24,16},{1,9},{9,1},{17,25},{25,17},{2,10},{10... | collective-permute-start | bytes 1376264 | tf_op jit(solution)/shard_map/ppermute | solution.py:460
  197.3 12.4 %collective-permute-start.24 = (bf16[2,64,1792]{2,1,0:T(8,128)(2,1)S(1)}, bf16[2,64,1792]{2,1,0:T(8,128)(2,1)}, u32[]{:S(2)}, u32[]{:S(2)}) collective-permute-start(bf16[2,64,1792]{2,1,0:T(8,128)(2,1)S(1)} %pad_maximum_fusion.17.refs_2_.refs_1_), channel_id=1, source_target_pairs={{0,16},{8,24},{16,0},{24,8},{1,17},{9,25},{17,1},{25,9},{2,18},{10... | collective-permute-start | bytes 1376264 | tf_op jit(solution)/shard_map/ppermute | solution.py:460
  202.1 10.4 %collective-permute-start.31 = (bf16[2,32,1792]{2,1,0:T(8,128)(2,1)}, bf16[2,32,1792]{2,1,0:T(8,128)(2,1)S(1)}, u32[]{:S(2)}, u32[]{:S(2)}) collective-permute-start(bf16[2,32,1792]{2,1,0:T(8,128)(2,1)} %slice.216), channel_id=1, source_target_pairs={{0,16},{8,24},{16,0},{24,8},{1,17},{9,25},{17,1},{25,9},{2,18},{10... | collective-permute-start | bytes 688136 | tf_op jit(solution)/shard_map/ppermute | solution.py:460
  216.5 16.9 %collective-permute-start.18 = (bf16[2,32,1792]{2,1,0:T(8,128)(2,1)S(1)}, bf16[2,32,1792]{2,1,0:T(8,128)(2,1)S(1)}, u32[]{:S(2)}, u32[]{:S(2)}) collective-permute-start(bf16[2,32,1792]{2,1,0:T(8,128)(2,1)S(1)} %slice.211), channel_id=1, source_target_pairs={{0,16},{8,24},{16,0},{24,8},{1,17},{9,25},{17,1},{25,9},{2,18},{10... | collective-permute-start | bytes 688136 | tf_op jit(solution)/shard_map/ppermute | solution.py:460
  220.0 13.4 %collective-permute-start.19 = (bf16[2,32,1792]{2,1,0:T(8,128)(2,1)S(1)}, bf16[2,32,1792]{2,1,0:T(8,128)(2,1)S(1)}, u32[]{:S(2)}, u32[]{:S(2)}) collective-permute-start(bf16[2,32,1792]{2,1,0:T(8,128)(2,1)S(1)} %slice.212), channel_id=1, source_target_pairs={{0,8},{8,0},{16,24},{24,16},{1,9},{9,1},{17,25},{25,17},{2,10},{10... | collective-permute-start | bytes 688136 | tf_op jit(solution)/shard_map/ppermute | solution.py:460
  240.0 13.2 %collective-permute-start.33 = (f32[16,64]{1,0:T(8,128)S(1)}, f32[16,64]{1,0:T(8,128)S(1)}, u32[]{:S(2)}, u32[]{:S(2)}) collective-permute-start(f32[16,64]{1,0:T(8,128)S(1)} %get-tuple-element.276), channel_id=1, source_target_pairs={{0,8},{8,0},{16,24},{24,16},{1,9},{9,1},{17,25},{25,17},{2,10},{10... | collective-permute-start | bytes 12296 | tf_op jit(solution)/shard_map/ppermute | solution.py:460
  241.5 11.7 %collective-permute-start.34 = (f32[16,64]{1,0:T(8,128)S(1)}, f32[16,64]{1,0:T(8,128)S(1)}, u32[]{:S(2)}, u32[]{:S(2)}) collective-permute-start(f32[16,64]{1,0:T(8,128)S(1)} %get-tuple-element.275), channel_id=1, source_target_pairs={{0,16},{8,24},{16,0},{24,8},{1,17},{9,25},{17,1},{25,9},{2,18},{10... | collective-permute-start | bytes 12296 | tf_op jit(solution)/shard_map/ppermute | solution.py:460
  242.5 10.7 %collective-permute-start.35 = (f32[16,64]{1,0:T(8,128)S(1)}, f32[16,64]{1,0:T(8,128)S(1)}, u32[]{:S(2)}, u32[]{:S(2)}) collective-permute-start(f32[16,64]{1,0:T(8,128)S(1)} %get-tuple-element.274), channel_id=1, source_target_pairs={{0,24},{8,16},{16,8},{24,0},{1,25},{9,17},{17,9},{25,1},{2,26},{10... | collective-permute-start | bytes 12296 | tf_op jit(solution)/shard_map/ppermute | solution.py:460
  (33 other events, 419.4 us)
